TPU v7x, 512 devices: a whole 4x4x16 slice. The times are simulated.
512 devices in a mesh: sec: 8 (over y, core), fsdp: 64 (over z, x).
Axes of the slice: x: 4, y: 4, z: 16, core: 2. Of those that a mesh axis runs over, the one named last changes fastest.
Arguments:
- tokens: bfloat16 [16384, 2048], P('fsdp', 'sec'), may hold values from -6 to 6
- routes: int32 [16384, 2], P('fsdp'), may hold values from 0 to 63, all different within a row; in each aligned block of 128 rows (0 to 127, 128 to 255, ...) at most 8 rows name the same one
- gate_weights: float32 [16384, 2], P('fsdp'), may hold values from 0.1 to 1
- pad_mask: int32 [16384], P('fsdp'), may hold values 0 or 1
- expand_weight: bfloat16 [64, 2048, 4096], P('fsdp', None, 'sec'), may hold values from -0.125 to 0.125
- shrink_weight: bfloat16 [64, 4096, 2048], P('fsdp', 'sec'), may hold values from -0.125 to 0.125
Outputs:
- mixed: bfloat16 [16384, 2048], P('fsdp', 'sec')
Inputs may be any that keep to these rules, and one draw needn't show every extreme that they name: `routes`: in each aligned block of 128 rows no expert is named by more than 8 rows, and the two experts of a row differ.
All inputs are finite; a program needn't handle non-finite values. No bound on the sum of `pad_mask` on one device may be relied on, other than what follows from the above.
Results may differ from a plain program's by a relative error of at most 0.019.
Values may be sent and summed in bfloat16 or wider, within the bound.
A program may use at most 64 MiB of HBM per device.

v0:
```python
import jax
import jax.numpy as jnp
from jax import lax
from jax.sharding import PartitionSpec as P

BLOCK = 128


def slot_targets(route_rows, experts, most, block):
    flat_ids = route_rows.reshape(-1)
    count = flat_ids.shape[0]
    top_k = route_rows.shape[1]
    onehot = (flat_ids[:, None] == jnp.arange(experts, dtype=jnp.int32)[None, :]).astype(jnp.int32)
    blocks = count // (top_k * block)
    running = jnp.cumsum(onehot.reshape(blocks, top_k * block, experts), axis=1).reshape(
        count, experts
    )
    rank_in = jnp.sum(onehot * running, axis=1) - 1
    block_ids = jnp.arange(count, dtype=jnp.int32) // (top_k * block)
    capacity = blocks * most
    return flat_ids * capacity + block_ids * most + rank_in


def shards(tokens, routes, gate_weights, pad_mask, expand_weight, shrink_weight):
    experts = lax.axis_size("fsdp")
    most = 4 * BLOCK // experts
    top_k = routes.shape[1]
    capacity = tokens.shape[0] // BLOCK * most
    targets = slot_targets(routes, experts, most, BLOCK)
    whole = lax.all_gather(tokens, "sec", axis=1, tiled=True)
    filled = jnp.zeros((experts * capacity, whole.shape[1]), jnp.bfloat16)
    filled = filled.at[targets].set(jnp.repeat(whole, top_k, axis=0))
    arrived = lax.all_to_all(
        filled.reshape(experts, capacity, whole.shape[1]),
        "fsdp",
        split_axis=0,
        concat_axis=0,
        tiled=True,
    )
    expert_rows = arrived.reshape(-1, arrived.shape[2])
    hidden = jnp.maximum(
        jnp.dot(expert_rows, expand_weight[0], preferred_element_type=jnp.float32), 0.0
    ).astype(jnp.bfloat16)
    partial_out = jnp.dot(hidden, shrink_weight[0], preferred_element_type=jnp.float32)
    summed = lax.psum_scatter(
        partial_out.astype(jnp.bfloat16), "sec", scatter_dimension=1, tiled=True
    )
    feature_share = summed.shape[1]
    returned = lax.all_to_all(
        summed.reshape(experts, capacity, feature_share),
        "fsdp",
        split_axis=0,
        concat_axis=0,
        tiled=True,
    )
    picked = (
        returned.reshape(-1, feature_share)[targets]
        .astype(jnp.float32)
        .reshape(-1, top_k, feature_share)
    )
    scale = gate_weights * pad_mask.astype(jnp.float32)[:, None]
    return jnp.sum(picked * scale[:, :, None], axis=1).astype(jnp.bfloat16)


def solution(mesh):
    in_specs = (
        P("fsdp", "sec"),
        P("fsdp", None),
        P("fsdp", None),
        P("fsdp"),
        P("fsdp", None, "sec"),
        P("fsdp", "sec", None),
    )
    out_specs = P("fsdp", "sec")
    return jax.shard_map(shards, mesh=mesh, in_specs=in_specs, out_specs=out_specs, check_vma=False)
```

profile of v0, /device:TPU:25, one launch (start us, length us, event | category | flops | bytes accessed | tf_op | source)
XLA Modules:
  0.0 369.1 jit_solution(14973955462616302387)
XLA Ops:
  6.5 0.0 copy-start
  6.5 0.0 all-gather.2.cloned.1.call-start
  6.5 0.7 all-gather.2.cloned.1.call-update
  7.3 0.0 reduce-scatter.2.cloned.1.call-start
  7.3 0.8 copy.9
  8.1 0.1 eq.31
  8.3 0.1 eq.27
  8.4 1.2 reduce-window.6
  9.6 0.2 slice_reduce_fusion
  9.9 0.1 fusion.10
  10.1 0.7 broadcast_multiply_fusion.1
  10.8 0.1 copy.8
  10.9 0.1 mul.48
  11.1 33.4 %all-gather.2.cloned.1.call-done = bf16[256,2048]{1,0:T(8,128)(2,1)} async-done(((bf16[256,256]{1,0:T(8,128)(2,1)}), bf16[256,2048]{1,0:T(8,128)(2,1)}) %all-gather.2.cloned.1.call-update) | async-done | bytes 1048592 | tf_op jit(solution)/shard_map/all_gather | solution.py:30
  44.5 3.8 %broadcast_in_dim.5 = bf16[256,2,2048]{2,1,0:T(2,128)(2,1)} broadcast(bf16[256,2048]{1,0:T(8,128)(2,1)} %all-gather.2.cloned.1.call-done), dimensions={0,2} | broadcast | bytes 3145728 | tf_op jit(solution)/shard_map/broadcast_in_dim | solution.py:32
  48.3 4.1 %reshape.149 = bf16[512,2048]{1,0:T(8,128)(2,1)} reshape(bf16[256,2,2048]{2,1,0:T(2,128)(2,1)} %broadcast_in_dim.5) | data formatting | bytes 4194304 | tf_op jit(solution)/shard_map/reshape | solution.py:32
  52.4 7.2 %scatter_custom_fusion = bf16[1024,2048]{1,0:T(8,128)(2,1)} fusion(s32[512]{0:T(512)S(1)} %bitcast.40, bf16[512,2048]{1,0:T(8,128)(2,1)} %reshape.149, bf16[]{:T(256)} %constant.27.clone.1), kind=kCustom, calls=%fused_computation.7 | custom fusion | bytes 4194816 | tf_op jit(solution)/shard_map/scatter | solution.py:32
  59.6 202.4 %all_to_all.10 = bf16[64,16,2048]{2,1,0:T(8,128)(2,1)} all-to-all(bf16[64,16,2048]{2,1,0:T(8,128)(2,1)} %bitcast.36), channel_id=1, replica_groups=mesh['sec'=8,'fsdp'=64] {'fsdp'}, dimensions={0} | all-to-all | bytes 8388608 | tf_op jit(solution)/shard_map/all_to_all | solution.py:33
  262.0 0.0 copy-done
  262.0 9.3 %convolution_convert_fusion = bf16[1024,2048]{1,0:T(8,128)(2,1)} fusion(bf16[1,512,2048]{2,1,0:T(8,128)(2,1)S(1)} %copy-done, bf16[1024,2048]{1,0:T(8,128)(2,1)} %bitcast.38, bf16[1,2048,512]{2,1,0:T(8,128)(2,1)} %param.10), kind=kOutput, calls=%fused_computation.2 | convolution fusion | flops 4298113024 | bytes 12582912 | tf_op jit(solution)/shard_map/dot_general | solution.py:44
  271.3 0.0 copy-start.2
  271.3 0.0 copy-start.1
  271.3 0.0 reduce-scatter.2.cloned.1.call-update
  271.4 40.2 %reduce-scatter.2.cloned.1.call-done = bf16[1024,256]{1,0:T(8,128)(2,1)} async-done(((bf16[1024,2048]{1,0:T(8,128)(2,1)}), bf16[1024,256]{1,0:T(8,128)(2,1)}) %reduce-scatter.2.cloned.1.call-update) | async-done | bytes 524304 | tf_op jit(solution)/shard_map/reduce_scatter | solution.py:45
  311.6 14.5 %all-to-all-start.1 = ((bf16[64,16,256]{2,1,0:T(8,128)(2,1)}), bf16[64,16,256]{2,1,0:T(8,128)(2,1)S(1)}, u32[]{:S(2)}, u32[]{:S(2)}) async-start(bf16[64,16,256]{2,1,0:T(8,128)(2,1)} %bitcast.39), calls=%async_computation.2 | async-start | bytes 1048576 | tf_op jit(solution)/shard_map/all_to_all | solution.py:49
  326.1 0.0 copy-done.2
  326.1 0.0 copy-done.1
  326.2 0.1 copy.12
  326.3 32.3 %all-to-all-done.1 = bf16[64,16,256]{2,1,0:T(8,128)(2,1)S(1)} async-done(((bf16[64,16,256]{2,1,0:T(8,128)(2,1)}), bf16[64,16,256]{2,1,0:T(8,128)(2,1)S(1)}, u32[]{:S(2)}, u32[]{:S(2)}) %all-to-all-start.1) | async-done | bytes 524320 | tf_op jit(solution)/shard_map/all_to_all | solution.py:49
  358.6 1.9 gather_fusion
  360.6 0.3 reshape.136
  360.8 1.4 multiply_reduce_fusion
  (9 shorter events, 0.1 us)
Async XLA Ops:
  6.5 255.5 %copy-start = (bf16[1,512,2048]{2,1,0:T(8,128)(2,1)S(1)}, bf16[1,512,2048]{2,1,0:T(8,128)(2,1)}, u32[]{:S(2)}) copy-start(bf16[1,512,2048]{2,1,0:T(8,128)(2,1)} %param.11) | copy-start | bytes 6291460
  6.5 37.9 %all-gather.2.cloned.1.call-start = ((), (), s32[]{:S(2)}) async-start(), calls=%async_computation.3 | async-start | bytes 1179648 | tf_op jit(solution)/shard_map/all_gather | solution.py:30
  7.3 304.3 %reduce-scatter.2.cloned.1.call-start = ((), (), s32[]{:S(2)}) async-start(), calls=%async_computation.4 | async-start | bytes 4718592 | tf_op jit(solution)/shard_map/reduce_scatter | solution.py:45
  271.3 54.8 %copy-start.2 = (s32[256]{0:T(256)S(1)}, s32[256]{0:T(256)}, u32[]{:S(2)}) copy-start(s32[256]{0:T(256)} %param.9) | copy-start | bytes 3076
  271.3 54.8 %copy-start.1 = (f32[256,2]{0,1:T(2,128)S(1)}, f32[256,2]{0,1:T(2,128)}, u32[]{:S(2)}) copy-start(f32[256,2]{0,1:T(2,128)} %param.8) | copy-start | bytes 6148
  311.6 47.0 %all-to-all-start.1 = ((bf16[64,16,256]{2,1,0:T(8,128)(2,1)}), bf16[64,16,256]{2,1,0:T(8,128)(2,1)S(1)}, u32[]{:S(2)}, u32[]{:S(2)}) async-start(bf16[64,16,256]{2,1,0:T(8,128)(2,1)} %bitcast.39), calls=%async_computation.2 | async-start | bytes 1048576 | tf_op jit(solution)/shard_map/all_to_all | solution.py:49
Sparse Core Ops, SparseCore 0:
  9.5 34.9 all-gather.1
  271.5 40.0 reduce-scatter.1
where the time goes:
time: 369 us
  blocking collectives  202 us (55%)
  waiting for transfers between devices  107 us (29%)
  local copies, waits for them, and re-layouts  19.1 us (5%)
  starting transfers between devices  14.6 us (4%)
  between operations  13.5 us (4%)
  matrix products  9.29 us (3%)
    all_to_all x1, blocking collectives, shards(): lax.all_to_all(filled.reshape(experts, capacity, whole.shape[1]), 'fsdp',...  202 us
    reduce_scatter x1, waiting for transfers between devices, shards(): lax.psum_scatter(partial_out.astype(jnp.bfloat16), 'sec', scatter_dimensi...  40.2 us
    all_gather x1, waiting for transfers between devices, shards(): whole = lax.all_gather(tokens, 'sec', axis=1, tiled=True)  33.4 us
    all_to_all x1, waiting for transfers between devices, shards(): lax.all_to_all(summed.reshape(experts, capacity, feature_share), 'fsdp',...  32.3 us
    all_to_all x1, starting transfers between devices, shards(): lax.all_to_all(summed.reshape(experts, capacity, feature_share), 'fsdp',...  14.5 us
    dot_general x1, matrix products, shards(): jnp.dot(hidden, shrink_weight[0], preferred_element_type=jnp.float32)  9.29 us
  transfers between devices with their start and end apart: 3, of which 3 were waited for; matrix products, arithmetic and copies ran while one was open for 1% of the time, Pallas kernels for 0%

commit v1 on v0

v1 whole, which is shorter than its diff:
```python
import jax
import jax.numpy as jnp
from jax import lax
from jax.experimental import pallas as pl
from jax.experimental.pallas import tpu as pltpu
from jax.sharding import PartitionSpec as P

MESH = pl.DeviceIdType.MESH
NZ, NX, NY = 16, 4, 4
SLOTS = 16
SHARE = 256
ROWS = NZ * NX * SLOTS
ORDER = (0, 1, 15, 2, 8, 9, 7, 10, 6, 11, 5, 12, 4, 13, 3, 14)
PER = 2
NB = NZ // PER
B = PER * NX * SLOTS
BF = jnp.bfloat16
F32 = jnp.float32


def wait_for(ref, sem):
    pltpu.make_async_copy(ref, ref, sem).wait()


def kernel(tok_hbm, routes_hbm, gates_hbm, mask_hbm, w1_hbm, w2_hbm, out, tok, routes, gates, mask, w1, w2, filled, g, part, sibp, cs, yrecv,
           eo, ret, qhi, qlo, w_sem, d_send, d_recv, a_send, a_recv, s_send, s_recv, p_send, p_recv,
           y_send, y_recv, r_send, r_recv):
    sec = lax.axis_index("sec")
    fs = lax.axis_index("fsdp")
    y, c = sec // 2, sec % 2
    z, x = fs // NX, fs % NX
    sib = (y * 2 + (1 - c), fs)

    def at(dz, dx):
        return (sec, (z + dz) % NZ * NX + (x + dx) % NX)

    def at_y(dy):
        return ((y + dy) % NY * 2 + c, fs)

    pairs = ((routes_hbm, routes), (tok_hbm, tok), (gates_hbm, gates), (mask_hbm, mask))
    loads = [pltpu.make_async_copy(src, dst, w_sem.at[2 + i]) for i, (src, dst) in enumerate(pairs)]
    for load in loads:
        load.start()

    barrier = pltpu.get_barrier_semaphore()
    partners = [at(ORDER[p], dx) for p in reversed(range(NZ)) for dx in range(NX) if (ORDER[p], dx) != (0, 0)]
    partners += [at_y(1), at_y(2), at_y(3), sib]
    for partner in partners:
        pl.semaphore_signal(barrier, inc=1, device_id=partner, device_id_type=MESH)

    load1 = pltpu.make_async_copy(w1_hbm.at[0], w1, w_sem.at[0])
    load2 = pltpu.make_async_copy(w2_hbm.at[0], w2, w_sem.at[1])
    load1.start()
    load2.start()
    for load in loads[:2]:
        load.wait()

    ids = routes[...]
    expert = lax.broadcasted_iota(jnp.int32, (NZ * NX, 256), 0)
    named = [(expert == ids[k:k + 1, :]).astype(F32) for k in range(2)]
    row = lax.broadcasted_iota(jnp.int32, (256, 256), 0)
    col = lax.broadcasted_iota(jnp.int32, (256, 256), 1)
    earlier = ((row < col) & (row // 128 == col // 128)).astype(BF)
    before = jnp.dot((named[0] + named[1]).astype(BF), earlier, preferred_element_type=F32)
    away = (z - (ids >> 2)) & (NZ - 1)
    place = jnp.zeros_like(ids)
    for p, r in enumerate(ORDER):
        place = jnp.where(away == r, p, place)
    half = lax.broadcasted_iota(jnp.int32, (1, 256), 1) // 128
    target = []
    for k in range(2):
        rank = jnp.sum(named[k] * before, axis=0, keepdims=True).astype(jnp.int32)
        target.append(place[k:k + 1, :] * (NX * SLOTS) + (ids[k:k + 1, :] & (NX - 1)) * SLOTS + half * 8 + rank)
    slot = lax.broadcasted_iota(jnp.int32, (ROWS, 256), 0)
    pick = ((slot == target[0]) | (slot == target[1])).astype(BF)
    filled[...] = jnp.dot(pick, tok[...], preferred_element_type=F32).astype(BF).reshape(NZ * NX, SLOTS, SHARE)

    pl.semaphore_wait(barrier, len(partners))

    def rows(b):
        return pl.ds(b * B, B)

    for p, r in enumerate(ORDER):
        for dx in range(NX):
            there = (x + dx) % NX
            src = filled.at[p * NX + there]
            dst = g.at[c, y, pl.ds(pl.multiple_of((p * NX + x) * SLOTS, SLOTS), SLOTS)]
            if (r, dx) == (0, 0):
                pltpu.make_async_copy(src, dst, d_recv.at[p // PER]).start()
            else:
                pltpu.make_async_remote_copy(
                    src_ref=src, dst_ref=dst, send_sem=d_send, recv_sem=d_recv.at[p // PER],
                    device_id=at(NZ - r, dx), device_id_type=MESH).start()

    for load in loads[2:]:
        load.wait()
    scale = gates[...] * mask[...].astype(F32)
    lanes = jnp.concatenate([target[0].astype(F32), target[1].astype(F32), scale, jnp.zeros((124, 256), F32)], axis=0)
    sides = lanes.T
    column = lax.broadcasted_iota(jnp.int32, (256, ROWS), 1)
    q = jnp.where(column == sides[:, 0:1].astype(jnp.int32), sides[:, 2:3], 0.0)
    q = q + jnp.where(column == sides[:, 1:2].astype(jnp.int32), sides[:, 3:4], 0.0)
    high = q.astype(BF)
    qhi[...] = high
    qlo[...] = (q - high.astype(F32)).astype(BF)

    def gather(b):
        wait_for(g.at[c, y, rows(b)], d_recv.at[b])
        own = g.at[c, y, rows(b)]
        for dy in (2, 1, 3):
            pltpu.make_async_remote_copy(
                src_ref=own, dst_ref=own, send_sem=a_send, recv_sem=a_recv.at[b, dy - 1],
                device_id=at_y(dy), device_id_type=MESH).start()
        pltpu.make_async_remote_copy(
            src_ref=own, dst_ref=own, send_sem=s_send, recv_sem=s_recv.at[b],
            device_id=sib, device_id_type=MESH).start()

    def share(b):
        for dy in (1, 3, 2):
            block = g.at[c, (y + NY - dy) % NY, rows(b)]
            wait_for(block, a_recv.at[b, dy - 1])
            pltpu.make_async_remote_copy(
                src_ref=block, dst_ref=block, send_sem=s_send, recv_sem=s_recv.at[b],
                device_id=sib, device_id_type=MESH).start()

    def feed(b):
        wait_for(g.at[1 - c, :, rows(b)], s_recv.at[b])
        if b == 0:
            load1.wait()
            load2.wait()
        xs = jnp.concatenate([g[s % 2, s // 2, rows(b), :] for s in range(8)], axis=1)
        hidden = jnp.maximum(jnp.dot(xs, w1[...], preferred_element_type=F32), 0.0).astype(BF)
        outs = jnp.dot(hidden, w2[...], preferred_element_type=F32).astype(BF)
        for s in range(8):
            part[b, s % 2, s // 2] = outs[:, s * SHARE:(s + 1) * SHARE]
        pltpu.make_async_remote_copy(
            src_ref=part.at[b, 1 - c], dst_ref=sibp.at[b], send_sem=p_send, recv_sem=p_recv.at[b],
            device_id=sib, device_id_type=MESH).start()

    def scatter(b):
        wait_for(sibp.at[b], p_recv.at[b])
        for dy in (2, 1, 3):
            there = (y + dy) % NY
            cs[b, dy - 1] = (part[b, c, there].astype(F32) + sibp[b, there].astype(F32)).astype(BF)
            pltpu.make_async_remote_copy(
                src_ref=cs.at[b, dy - 1], dst_ref=yrecv.at[b, dy - 1], send_sem=y_send,
                recv_sem=y_recv.at[b, dy - 1], device_id=at_y(dy), device_id_type=MESH).start()

    def give_back(b):
        total = part[b, c, y].astype(F32) + sibp[b, y].astype(F32)
        for dy in (1, 3, 2):
            wait_for(yrecv.at[b, dy - 1], y_recv.at[b, dy - 1])
            total = total + yrecv[b, dy - 1].astype(F32)
        eo[pl.ds(b * PER * NX, PER * NX)] = total.astype(BF).reshape(PER * NX, SLOTS, SHARE)
        for p in range(b * PER, (b + 1) * PER):
            for dx in range(NX):
                src = eo.at[p * NX + (x + dx) % NX]
                dst = ret.at[p * NX + x]
                if (ORDER[p], dx) == (0, 0):
                    pltpu.make_async_copy(src, dst, r_recv.at[b]).start()
                else:
                    pltpu.make_async_remote_copy(
                        src_ref=src, dst_ref=dst, send_sem=r_send, recv_sem=r_recv.at[b],
                        device_id=at(ORDER[p], dx), device_id_type=MESH).start()

    stages = (gather, share, feed, scatter, give_back)
    for step in range(NB + len(stages) - 1):
        for lag in reversed(range(len(stages))):
            if 0 <= step - lag < NB:
                stages[lag](step - lag)

    mixed = jnp.zeros((256, SHARE), F32)
    for b in range(NB):
        wait_for(ret.at[pl.ds(b * PER * NX, PER * NX)], r_recv.at[b])
        block = ret[pl.ds(b * PER * NX, PER * NX)].reshape(B, SHARE)
        mixed = mixed + jnp.dot(qhi[:, b * B:(b + 1) * B], block, preferred_element_type=F32)
        mixed = mixed + jnp.dot(qlo[:, b * B:(b + 1) * B], block, preferred_element_type=F32)
    out[...] = mixed.astype(BF)

    wait_for(filled.at[pl.ds(0, NZ * NX - 1)], d_send)
    wait_for(g.at[0, pl.ds(0, 3)], a_send)
    wait_for(g.at[0], s_send)
    wait_for(sibp, p_send)
    wait_for(cs, y_send)
    wait_for(eo.at[pl.ds(0, NZ * NX - 1)], r_send)


def shards(tokens, routes, gate_weights, pad_mask, expand_weight, shrink_weight):
    vmem = pl.BlockSpec(memory_space=pltpu.VMEM)
    hbm = pl.BlockSpec(memory_space=pltpu.HBM)
    dma = pltpu.SemaphoreType.DMA
    return pl.pallas_call(
        kernel,
        out_shape=jax.ShapeDtypeStruct((256, SHARE), BF),
        in_specs=[hbm] * 6,
        out_specs=vmem,
        scratch_shapes=[
            pltpu.VMEM((256, SHARE), BF),
            pltpu.VMEM((2, 256), jnp.int32),
            pltpu.VMEM((2, 256), F32),
            pltpu.VMEM((1, 256), jnp.int32),
            pltpu.VMEM((2048, 512), BF),
            pltpu.VMEM((512, 2048), BF),
            pltpu.VMEM((NZ * NX, SLOTS, SHARE), BF),
            pltpu.VMEM((2, NY, ROWS, SHARE), BF),
            pltpu.VMEM((NB, 2, NY, B, SHARE), BF),
            pltpu.VMEM((NB, NY, B, SHARE), BF),
            pltpu.VMEM((NB, 3, B, SHARE), BF),
            pltpu.VMEM((NB, 3, B, SHARE), BF),
            pltpu.VMEM((NZ * NX, SLOTS, SHARE), BF),
            pltpu.VMEM((NZ * NX, SLOTS, SHARE), BF),
            pltpu.VMEM((256, ROWS), BF),
            pltpu.VMEM((256, ROWS), BF),
            dma((6,)),
            dma,
            dma((NB,)),
            dma,
            dma((NB, 3)),
            dma,
            dma((NB,)),
            dma,
            dma((NB,)),
            dma,
            dma((NB, 3)),
            dma,
            dma((NB,)),
        ],
        compiler_params=pltpu.CompilerParams(
            collective_id=0, has_side_effects=True, vmem_limit_bytes=63 * 2**20),
        cost_estimate=pl.CostEstimate(flops=4 * ROWS * 2048 * 512, bytes_accessed=5 * 2**20, transcendentals=0),
        name="moe",
    )(tokens, routes.T, gate_weights.T, pad_mask.reshape(1, 256), expand_weight, shrink_weight)


def solution(mesh):
    in_specs = (
        P("fsdp", "sec"),
        P("fsdp", None),
        P("fsdp", None),
        P("fsdp"),
        P("fsdp", None, "sec"),
        P("fsdp", "sec", None),
    )
    out_specs = P("fsdp", "sec")
    return jax.shard_map(shards, mesh=mesh, in_specs=in_specs, out_specs=out_specs, check_vma=False)
```

time: 369 us -> 88.3 us (0.24)
  the two profiles are of different devices: /device:TPU:25 before, /device:TPU:32 now
where the time goes in v1:
time: 88.3 us; the launch traced here: 88.1 us
  Pallas kernels  86.6 us (98%)
  local copies, waits for them, and re-layouts  1.57 us (2%)
    pallas_call x1, Pallas kernels, shards(): pl.pallas_call(kernel, out_shape=jax.ShapeDtypeStruct((256, SHARE), BF),...  86.6 us

profile of v1, /device:TPU:32, one launch (start us, length us, event | category | flops | bytes accessed | tf_op | source)
XLA Modules:
  0.0 88.1 jit_solution(1563566794700460265)
XLA Ops:
  0.0 86.6 %moe.1 = bf16[256,256]{1,0:T(8,128)(2,1)} custom-call(bf16[256,256]{1,0:T(8,128)(2,1)} %tok_hbm.1, s32[2,256]{1,0:T(2,128)} %bitcast.3, f32[2,256]{1,0:T(2,128)} %bitcast.4, s32[1,256]{1,0:T(1,128)} %bitcast.5, bf16[1,2048,512]{2,1,0:T(8,128)(2,1)} %w1_hbm.1, bf16[1,512,2048]{2,1,0:T(8,128)(2,1)} %w2_hbm.1), custom_call_target="tpu_custom_call" | custom-call | flops 4294967296 | bytes 5242880 | tf_op jit(solution)/shard_map/moe/pallas_call | solution.py:192
  86.6 1.6 %copy.8 = bf16[256,256]{1,0:T(8,128)(2,1)} copy(bf16[256,256]{1,0:T(8,128)(2,1)} %moe.1) | data formatting | bytes 262144

commit v2 on v1

v2 whole, which is shorter than its diff:
```python
import jax
import jax.numpy as jnp
from jax import lax
from jax.experimental import pallas as pl
from jax.experimental.pallas import tpu as pltpu
from jax.sharding import PartitionSpec as P

MESH = pl.DeviceIdType.MESH
NZ, NX, NY = 16, 4, 4
SLOTS = 16
SHARE = 256
ROWS = NZ * NX * SLOTS
BLOCKS = ((0, 14, 15), (1,), (4,), (5, 11), (8,), (10,), (12,), (7,), (13, 3), (9,), (2,), (6,))
STEPS = (
    (0, 1), (0, 0), (0, 2), (1, 0), (1, 1), (2, 1), (0, 3), (3, 1), (1, 2), (2, 2), (0, 4), (0, 5), (0, 6),
    (3, 2), (1, 3), (2, 3), (2, 0), (0, 8), (5, 1), (0, 7), (1, 4), (2, 4), (3, 3), (0, 10), (1, 5), (2, 5),
    (5, 2), (1, 6), (0, 9), (3, 0), (3, 4), (1, 8), (0, 11), (1, 7), (2, 7), (5, 3), (3, 5), (1, 10), (3, 7),
    (2, 6), (4, 0), (1, 9), (2, 9), (5, 4), (2, 8), (3, 6), (3, 9), (1, 11), (2, 11), (5, 5), (2, 10), (3, 8),
    (5, 7), (3, 11), (5, 0), (4, 6), (3, 10), (5, 9), (4, 8), (5, 11), (5, 6), (4, 10), (5, 8), (5, 10),
)
ORDER = sum(BLOCKS, ())
STEPS_FIRST = next(b for stage, b in STEPS if stage == 2)
NB = len(BLOCKS)
FIRST = tuple(sum(len(r) for r in BLOCKS[:b]) for b in range(NB + 1))
BLOCK_AT = tuple(b for b in range(NB) for _ in BLOCKS[b])
NEAR = 4
DIRECT = (0, 1, 1, 1, 1, 1, 0, 1, 0, 1, 0, 1)
EARLY = next(p for p in range(NZ) if min(ORDER[p], NZ - ORDER[p]) > NEAR)
BF = jnp.bfloat16
F32 = jnp.float32


def wait_for(ref, sem):
    pltpu.make_async_copy(ref, ref, sem).wait()


def kernel(tok_hbm, routes_hbm, gates_hbm, mask_hbm, w1_hbm, w2_hbm, out, tok, routes, gates, mask, w1, w2,
           filled, g, hown, hout, hsib, osum, cs, yrecv, hrecv, eo, ret, qhi, qlo, w_sem, w_send, w_recv, d_send,
           d_recv, a_send, a_recv, h_recv, p_send, p_recv, y_send, y_recv, e_recv, r_send, r_recv, far_in):
    sec = lax.axis_index("sec")
    fs = lax.axis_index("fsdp")
    y, c = sec // 2, sec % 2
    z, x = fs // NX, fs % NX
    sib = (y * 2 + (1 - c), fs)

    def at(dz, dx):
        return (sec, (z + dz) % NZ * NX + (x + dx) % NX)

    def at_y(dy):
        return ((y + dy) % NY * 2 + c, fs)

    barrier = pltpu.get_barrier_semaphore()
    partners = [at(dz, dx) for d in range(NEAR, -1, -1) for dz in sorted({d, (NZ - d) % NZ}) for dx in range(NX) if (dz, dx) != (0, 0)]
    partners += [at_y(1), at_y(2), at_y(3), sib]
    for partner in partners:
        pl.semaphore_signal(barrier, inc=1, device_id=partner, device_id_type=MESH)

    def strips(parity, to):
        for k in range(NY):
            start = pl.multiple_of((k * 2 + parity) * SHARE, SHARE)
            here = pl.ds(k * SHARE, SHARE)
            to(w1_hbm.at[0, pl.ds(start, SHARE)], w1.at[c, here], 0)
            to(w2_hbm.at[0, :, pl.ds(start, SHARE)], w2.at[c, :, here], 1)

    strips(c, lambda src, dst, k: pltpu.make_async_copy(src, dst, w_sem.at[k]).start())
    loads = [pltpu.make_async_copy(src, dst, w_sem.at[2 + i]) for i, (src, dst) in enumerate(
        ((routes_hbm, routes), (tok_hbm, tok), (gates_hbm, gates), (mask_hbm, mask)))]
    for load in loads:
        load.start()
    for load in loads[:2]:
        load.wait()

    ids = routes[...]
    expert = lax.broadcasted_iota(jnp.int32, (NZ * NX, 256), 0)
    named = [(expert == ids[k:k + 1, :]).astype(F32) for k in range(2)]
    row = lax.broadcasted_iota(jnp.int32, (256, 256), 0)
    col = lax.broadcasted_iota(jnp.int32, (256, 256), 1)
    earlier = ((row < col) & (row // 128 == col // 128)).astype(BF)
    before = jnp.dot((named[0] + named[1]).astype(BF), earlier, preferred_element_type=F32)
    away = (z - (ids >> 2)) & (NZ - 1)
    place = jnp.zeros_like(ids)
    for p, r in enumerate(ORDER):
        place = jnp.where(away == r, p, place)
    half = lax.broadcasted_iota(jnp.int32, (1, 256), 1) // 128
    target = []
    for k in range(2):
        rank = jnp.sum(named[k] * before, axis=0, keepdims=True).astype(jnp.int32)
        target.append(place[k:k + 1, :] * (NX * SLOTS) + (ids[k:k + 1, :] & (NX - 1)) * SLOTS + half * 8 + rank)
    slot = lax.broadcasted_iota(jnp.int32, (ROWS, 256), 0)
    pick = ((slot == target[0]) | (slot == target[1])).astype(BF)
    filled[...] = jnp.dot(pick, tok[...], preferred_element_type=F32).astype(BF).reshape(NZ * NX, SLOTS, SHARE)

    pl.semaphore_wait(barrier, len(partners))
    pl.semaphore_signal(far_in.at[0], inc=1, device_id=at(NEAR, 0), device_id_type=MESH)
    pl.semaphore_signal(far_in.at[1], inc=1, device_id=at(NZ - NEAR, 0), device_id_type=MESH)

    def rows(b):
        return pl.ds(FIRST[b] * NX * SLOTS, len(BLOCKS[b]) * NX * SLOTS)

    def chunks(b):
        return pl.ds(FIRST[b] * NX, len(BLOCKS[b]) * NX)

    def dispatch(places):
        for p in places:
            r = ORDER[p]
            for dx in range(NX):
                src = filled.at[p * NX + (x + dx) % NX]
                dst = g.at[y, pl.ds(pl.multiple_of((p * NX + x) * SLOTS, SLOTS), SLOTS)]
                if (r, dx) == (0, 0):
                    pltpu.make_async_copy(src, dst, d_recv.at[BLOCK_AT[p]]).start()
                else:
                    pltpu.make_async_remote_copy(
                        src_ref=src, dst_ref=dst, send_sem=d_send, recv_sem=d_recv.at[BLOCK_AT[p]],
                        device_id=at(NZ - r, dx), device_id_type=MESH).start()

    dispatch(range(EARLY))
    strips(1 - c, lambda src, dst, k: pltpu.make_async_remote_copy(
        src_ref=src, dst_ref=dst, send_sem=w_send.at[k], recv_sem=w_recv.at[k], device_id=sib,
        device_id_type=MESH).start())

    for load in loads[2:]:
        load.wait()
    scale = gates[...] * mask[...].astype(F32)
    lanes = jnp.concatenate([target[0].astype(F32), target[1].astype(F32), scale, jnp.zeros((124, 256), F32)], axis=0)
    sides = lanes.T
    column = lax.broadcasted_iota(jnp.int32, (256, ROWS), 1)
    q = jnp.where(column == sides[:, 0:1].astype(jnp.int32), sides[:, 2:3], 0.0)
    q = q + jnp.where(column == sides[:, 1:2].astype(jnp.int32), sides[:, 3:4], 0.0)
    high = q.astype(BF)
    qhi[...] = high
    qlo[...] = (q - high.astype(F32)).astype(BF)

    pl.semaphore_wait(far_in.at[0], 1)
    pl.semaphore_wait(far_in.at[1], 1)
    dispatch(range(EARLY, NZ))

    def send(src, dst, send_sem, recv_sem, device):
        pltpu.make_async_remote_copy(
            src_ref=src, dst_ref=dst, send_sem=send_sem, recv_sem=recv_sem, device_id=device,
            device_id_type=MESH).start()

    def first(b):
        return pl.ds(FIRST[b] * NX * SLOTS, len(BLOCKS[b]) * NX * SLOTS // 2)

    def second(b):
        half = len(BLOCKS[b]) * NX * SLOTS // 2
        return pl.ds(FIRST[b] * NX * SLOTS + half, half)

    up, down, across = (y + 1) % NY, (y + NY - 1) % NY, (y + 2) % NY

    def gather(b):
        own = g.at[y, rows(b)]
        wait_for(own, d_recv.at[b])
        send(own, own, a_send, a_recv.at[b, 0], at_y(1))
        send(own, own, a_send, a_recv.at[b, 1], at_y(3))
        if DIRECT[b]:
            send(own, own, a_send, h_recv.at[b, 0], at_y(2))

    def relay(b):
        for k, (origin, half, dy) in enumerate(((down, first(b), 1), (up, second(b), 3))):
            wait_for(g.at[origin, rows(b)], a_recv.at[b, k])
            if not DIRECT[b]:
                part_of = g.at[origin, half]
                send(part_of, part_of, a_send, h_recv.at[b, k], at_y(dy))

    def expand(b):
        if DIRECT[b]:
            wait_for(g.at[across, rows(b)], h_recv.at[b, 0])
        else:
            wait_for(g.at[across, first(b)], h_recv.at[b, 0])
            wait_for(g.at[across, second(b)], h_recv.at[b, 1])
        if b == STEPS_FIRST:
            wait_for(w1.at[c], w_sem.at[0])
            wait_for(w2.at[c], w_sem.at[1])
            wait_for(w1.at[1 - c], w_recv.at[0])
            wait_for(w2.at[1 - c], w_recv.at[1])
        xs = jnp.concatenate([g[k, rows(b), :] for k in range(NY)], axis=1)
        for j in range(2):
            units = jnp.dot(xs, w1[j], preferred_element_type=F32)
            hown[j, rows(b), :] = units
            hout[j, rows(b), :] = units.astype(BF)
        send(hout.at[:, rows(b)], hsib.at[:, rows(b)], p_send, p_recv.at[b], sib)

    def shrink(b):
        wait_for(hsib.at[:, rows(b)], p_recv.at[b])
        total = None
        for j in range(2):
            hidden = jnp.maximum(hown[j, rows(b), :] + hsib[j, rows(b), :].astype(F32), 0.0).astype(BF)
            term = jnp.dot(hidden, w2[j], preferred_element_type=F32)
            total = term if total is None else total + term
        for k in range(NY):
            osum[k, rows(b), :] = total[:, k * SHARE:(k + 1) * SHARE]
        cs[1, rows(b), :] = osum[across, rows(b), :].astype(BF)
        if DIRECT[b]:
            send(cs.at[1, rows(b)], hrecv.at[rows(b)], y_send, e_recv.at[b, 0], at_y(2))
            for k, (strip, dy) in enumerate(((up, 1), (down, 3))):
                cs[2 * k, rows(b), :] = osum[strip, rows(b), :].astype(BF)
                send(cs.at[2 * k, rows(b)], yrecv.at[k, rows(b)], y_send, y_recv.at[b, k], at_y(dy))
        else:
            send(cs.at[1, first(b)], hrecv.at[first(b)], y_send, e_recv.at[b, 0], at_y(1))
            send(cs.at[1, second(b)], hrecv.at[second(b)], y_send, e_recv.at[b, 1], at_y(3))

    def pass_on(b):
        if DIRECT[b]:
            return
        for k, (strip, here, other, dy) in enumerate(((up, first(b), second(b), 1), (down, second(b), first(b), 3))):
            cs[2 * k, other, :] = osum[strip, other, :].astype(BF)
            wait_for(hrecv.at[here], e_recv.at[b, k])
            cs[2 * k, here, :] = (osum[strip, here, :] + hrecv[here, :].astype(F32)).astype(BF)
            send(cs.at[2 * k, rows(b)], yrecv.at[k, rows(b)], y_send, y_recv.at[b, k], at_y(dy))

    def give_back(b):
        total = osum[y, rows(b), :]
        if DIRECT[b]:
            wait_for(hrecv.at[rows(b)], e_recv.at[b, 0])
            total = total + hrecv[rows(b), :].astype(F32)
        for k in range(2):
            wait_for(yrecv.at[k, rows(b)], y_recv.at[b, k])
            total = total + yrecv[k, rows(b), :].astype(F32)
        eo[chunks(b)] = total.astype(BF).reshape(len(BLOCKS[b]) * NX, SLOTS, SHARE)
        for p in range(FIRST[b], FIRST[b + 1]):
            for dx in range(NX):
                src = eo.at[p * NX + (x + dx) % NX]
                dst = ret.at[p * NX + x]
                if (ORDER[p], dx) == (0, 0):
                    pltpu.make_async_copy(src, dst, r_recv.at[b]).start()
                else:
                    pltpu.make_async_remote_copy(
                        src_ref=src, dst_ref=dst, send_sem=r_send, recv_sem=r_recv.at[b],
                        device_id=at(ORDER[p], dx), device_id_type=MESH).start()

    stages = (gather, relay, expand, shrink, pass_on, give_back)
    for stage, b in STEPS:
        stages[stage](b)

    mixed = jnp.zeros((256, SHARE), F32)
    for b in range(NB):
        wait_for(ret.at[chunks(b)], r_recv.at[b])
        block = ret[chunks(b)].reshape(len(BLOCKS[b]) * NX * SLOTS, SHARE)
        mixed = mixed + jnp.dot(qhi[:, rows(b)], block, preferred_element_type=F32)
        mixed = mixed + jnp.dot(qlo[:, rows(b)], block, preferred_element_type=F32)
    out[...] = mixed.astype(BF)

    wait_for(filled.at[pl.ds(0, NZ * NX - 1)], d_send)
    wait_for(g.at[pl.ds(0, 3)], a_send)
    wait_for(hout, p_send)
    wait_for(w1.at[0], w_send.at[0])
    wait_for(w2.at[0], w_send.at[1])
    wait_for(cs, y_send)
    wait_for(eo.at[pl.ds(0, NZ * NX - 1)], r_send)


def shards(tokens, routes, gate_weights, pad_mask, expand_weight, shrink_weight):
    vmem = pl.BlockSpec(memory_space=pltpu.VMEM)
    hbm = pl.BlockSpec(memory_space=pltpu.HBM)
    dma = pltpu.SemaphoreType.DMA
    return pl.pallas_call(
        kernel,
        out_shape=jax.ShapeDtypeStruct((256, SHARE), BF),
        in_specs=[hbm] * 6,
        out_specs=vmem,
        scratch_shapes=[
            pltpu.VMEM((256, SHARE), BF),
            pltpu.VMEM((2, 256), jnp.int32),
            pltpu.VMEM((2, 256), F32),
            pltpu.VMEM((1, 256), jnp.int32),
            pltpu.VMEM((2, NY * SHARE, 512), BF),
            pltpu.VMEM((2, 512, NY * SHARE), BF),
            pltpu.VMEM((NZ * NX, SLOTS, SHARE), BF),
            pltpu.VMEM((NY, ROWS, SHARE), BF),
            pltpu.VMEM((2, ROWS, 512), F32),
            pltpu.VMEM((2, ROWS, 512), BF),
            pltpu.VMEM((2, ROWS, 512), BF),
            pltpu.VMEM((NY, ROWS, SHARE), F32),
            pltpu.VMEM((3, ROWS, SHARE), BF),
            pltpu.VMEM((2, ROWS, SHARE), BF),
            pltpu.VMEM((ROWS, SHARE), BF),
            pltpu.VMEM((NZ * NX, SLOTS, SHARE), BF),
            pltpu.VMEM((NZ * NX, SLOTS, SHARE), BF),
            pltpu.VMEM((256, ROWS), BF),
            pltpu.VMEM((256, ROWS), BF),
            dma((6,)),
            dma((2,)),
            dma((2,)),
            dma,
            dma((NB,)),
            dma,
            dma((NB, 2)),
            dma((NB, 2)),
            dma,
            dma((NB,)),
            dma,
            dma((NB, 2)),
            dma((NB, 2)),
            dma,
            dma((NB,)),
            pltpu.SemaphoreType.REGULAR((2,)),
        ],
        compiler_params=pltpu.CompilerParams(
            collective_id=0, has_side_effects=True, vmem_limit_bytes=63 * 2**20),
        cost_estimate=pl.CostEstimate(flops=4 * ROWS * 2048 * 512, bytes_accessed=5 * 2**20, transcendentals=0),
        name="moe",
    )(tokens, routes.T, gate_weights.T, pad_mask.reshape(1, 256), expand_weight, shrink_weight)


def solution(mesh):
    in_specs = (
        P("fsdp", "sec"),
        P("fsdp", None),
        P("fsdp", None),
        P("fsdp"),
        P("fsdp", None, "sec"),
        P("fsdp", "sec", None),
    )
    out_specs = P("fsdp", "sec")
    return jax.shard_map(shards, mesh=mesh, in_specs=in_specs, out_specs=out_specs, check_vma=False)
```

time: 88.3 us -> 80.1 us (0.907)
  the two profiles are of different devices: /device:TPU:32 before, /device:TPU:64 now
where the time goes in v2:
time: 80.1 us; the launch traced here: 80 us
  Pallas kernels  78.4 us (98%)
  local copies, waits for them, and re-layouts  1.57 us (2%)
    pallas_call x1, Pallas kernels, shards(): pl.pallas_call(kernel, out_shape=jax.ShapeDtypeStruct((256, SHARE), BF),...  78.4 us

profile of v2, /device:TPU:64, one launch (start us, length us, event | category | flops | bytes accessed | tf_op | source)
XLA Modules:
  0.0 80.0 jit_solution(14975765311072283214)
XLA Ops:
  0.0 78.4 %moe.1 = bf16[256,256]{1,0:T(8,128)(2,1)} custom-call(bf16[256,256]{1,0:T(8,128)(2,1)} %tok_hbm.1, s32[2,256]{1,0:T(2,128)} %bitcast.3, f32[2,256]{1,0:T(2,128)} %bitcast.4, s32[1,256]{1,0:T(1,128)} %bitcast.5, bf16[1,2048,512]{2,1,0:T(8,128)(2,1)} %w1_hbm.1, bf16[1,512,2048]{2,1,0:T(8,128)(2,1)} %w2_hbm.1), custom_call_target="tpu_custom_call" | custom-call | flops 4294967296 | bytes 5242880 | tf_op jit(solution)/shard_map/moe/pallas_call | solution.py:257
  78.4 1.6 %copy.8 = bf16[256,256]{1,0:T(8,128)(2,1)} copy(bf16[256,256]{1,0:T(8,128)(2,1)} %moe.1) | data formatting | bytes 262144

commit v3 on v2

--- a/solution.py
+++ b/solution.py
@@ -10,13 +10,13 @@
 SLOTS = 16
 SHARE = 256
 ROWS = NZ * NX * SLOTS
-BLOCKS = ((0, 14, 15), (1,), (4,), (5, 11), (8,), (10,), (12,), (7,), (13, 3), (9,), (2,), (6,))
+BLOCKS = ((2,), (4,), (12,), (8,), (14,), (0, 1), (7, 9), (6, 11), (13, 3, 15), (5,), (10,))
 STEPS = (
-    (0, 1), (0, 0), (0, 2), (1, 0), (1, 1), (2, 1), (0, 3), (3, 1), (1, 2), (2, 2), (0, 4), (0, 5), (0, 6),
-    (3, 2), (1, 3), (2, 3), (2, 0), (0, 8), (5, 1), (0, 7), (1, 4), (2, 4), (3, 3), (0, 10), (1, 5), (2, 5),
-    (5, 2), (1, 6), (0, 9), (3, 0), (3, 4), (1, 8), (0, 11), (1, 7), (2, 7), (5, 3), (3, 5), (1, 10), (3, 7),
-    (2, 6), (4, 0), (1, 9), (2, 9), (5, 4), (2, 8), (3, 6), (3, 9), (1, 11), (2, 11), (5, 5), (2, 10), (3, 8),
-    (5, 7), (3, 11), (5, 0), (4, 6), (3, 10), (5, 9), (4, 8), (5, 11), (5, 6), (4, 10), (5, 8), (5, 10),
+    (0, 0), (0, 2), (0, 1), (0, 5), (1, 0), (2, 0), (0, 4), (1, 2), (2, 2), (0, 3), (1, 1), (2, 1), (1, 5),
+    (3, 0), (1, 4), (3, 2), (3, 1), (0, 6), (1, 3), (2, 3), (2, 5), (2, 4), (0, 7), (3, 3), (5, 0), (5, 2),
+    (5, 1), (0, 8), (3, 4), (0, 9), (1, 6), (2, 6), (1, 7), (0, 10), (3, 5), (1, 8), (3, 6), (4, 4), (5, 3),
+    (1, 9), (2, 9), (2, 7), (4, 5), (1, 10), (2, 10), (2, 8), (3, 9), (3, 7), (5, 6), (3, 10), (5, 4), (3, 8),
+    (5, 5), (5, 9), (4, 7), (5, 10), (4, 8), (5, 7), (5, 8),
 )
 ORDER = sum(BLOCKS, ())
 STEPS_FIRST = next(b for stage, b in STEPS if stage == 2)
@@ -24,7 +24,7 @@
 FIRST = tuple(sum(len(r) for r in BLOCKS[:b]) for b in range(NB + 1))
 BLOCK_AT = tuple(b for b in range(NB) for _ in BLOCKS[b])
 NEAR = 4
-DIRECT = (0, 1, 1, 1, 1, 1, 0, 1, 0, 1, 0, 1)
+DIRECT = (1, 1, 1, 1, 0, 0, 1, 0, 0, 1, 1)
 EARLY = next(p for p in range(NZ) if min(ORDER[p], NZ - ORDER[p]) > NEAR)
 BF = jnp.bfloat16
 F32 = jnp.float32
@@ -49,6 +49,11 @@
     def at_y(dy):
         return ((y + dy) % NY * 2 + c, fs)
 
+    loads = [pltpu.make_async_copy(src, dst, w_sem.at[2 + i]) for i, (src, dst) in enumerate(
+        ((routes_hbm, routes), (tok_hbm, tok), (gates_hbm, gates), (mask_hbm, mask)))]
+    for load in loads:
+        load.start()
+
     barrier = pltpu.get_barrier_semaphore()
     partners = [at(dz, dx) for d in range(NEAR, -1, -1) for dz in sorted({d, (NZ - d) % NZ}) for dx in range(NX) if (dz, dx) != (0, 0)]
     partners += [at_y(1), at_y(2), at_y(3), sib]
@@ -62,20 +67,15 @@
             to(w1_hbm.at[0, pl.ds(start, SHARE)], w1.at[c, here], 0)
             to(w2_hbm.at[0, :, pl.ds(start, SHARE)], w2.at[c, :, here], 1)
 
-    strips(c, lambda src, dst, k: pltpu.make_async_copy(src, dst, w_sem.at[k]).start())
-    loads = [pltpu.make_async_copy(src, dst, w_sem.at[2 + i]) for i, (src, dst) in enumerate(
-        ((routes_hbm, routes), (tok_hbm, tok), (gates_hbm, gates), (mask_hbm, mask)))]
-    for load in loads:
-        load.start()
+    row = lax.broadcasted_iota(jnp.int32, (256, 256), 0)
+    col = lax.broadcasted_iota(jnp.int32, (256, 256), 1)
+    earlier = ((row < col) & (row // 128 == col // 128)).astype(BF)
     for load in loads[:2]:
         load.wait()
 
     ids = routes[...]
     expert = lax.broadcasted_iota(jnp.int32, (NZ * NX, 256), 0)
     named = [(expert == ids[k:k + 1, :]).astype(F32) for k in range(2)]
-    row = lax.broadcasted_iota(jnp.int32, (256, 256), 0)
-    col = lax.broadcasted_iota(jnp.int32, (256, 256), 1)
-    earlier = ((row < col) & (row // 128 == col // 128)).astype(BF)
     before = jnp.dot((named[0] + named[1]).astype(BF), earlier, preferred_element_type=F32)
     away = (z - (ids >> 2)) & (NZ - 1)
     place = jnp.zeros_like(ids)
@@ -86,10 +86,13 @@
     for k in range(2):
         rank = jnp.sum(named[k] * before, axis=0, keepdims=True).astype(jnp.int32)
         target.append(place[k:k + 1, :] * (NX * SLOTS) + (ids[k:k + 1, :] & (NX - 1)) * SLOTS + half * 8 + rank)
-    slot = lax.broadcasted_iota(jnp.int32, (ROWS, 256), 0)
-    pick = ((slot == target[0]) | (slot == target[1])).astype(BF)
-    filled[...] = jnp.dot(pick, tok[...], preferred_element_type=F32).astype(BF).reshape(NZ * NX, SLOTS, SHARE)
-
+    def fill(start, stop):
+        slot = lax.broadcasted_iota(jnp.int32, ((stop - start) * NX * SLOTS, 256), 0) + start * NX * SLOTS
+        pick = ((slot == target[0]) | (slot == target[1])).astype(BF)
+        held = jnp.dot(pick, tok[...], preferred_element_type=F32).astype(BF)
+        filled[pl.ds(start * NX, (stop - start) * NX)] = held.reshape((stop - start) * NX, SLOTS, SHARE)
+
+    fill(0, EARLY)
     pl.semaphore_wait(barrier, len(partners))
     pl.semaphore_signal(far_in.at[0], inc=1, device_id=at(NEAR, 0), device_id_type=MESH)
     pl.semaphore_signal(far_in.at[1], inc=1, device_id=at(NZ - NEAR, 0), device_id_type=MESH)
@@ -114,9 +117,12 @@
                         device_id=at(NZ - r, dx), device_id_type=MESH).start()
 
     dispatch(range(EARLY))
+    strips(c, lambda src, dst, k: pltpu.make_async_copy(src, dst, w_sem.at[k]).start())
     strips(1 - c, lambda src, dst, k: pltpu.make_async_remote_copy(
         src_ref=src, dst_ref=dst, send_sem=w_send.at[k], recv_sem=w_recv.at[k], device_id=sib,
         device_id_type=MESH).start())
+
+    fill(EARLY, NZ)
 
     for load in loads[2:]:
         load.wait()

time: 80.1 us -> 79.5 us (level)
  the two profiles are of different devices: /device:TPU:64 before, /device:TPU:32 now
where the time goes in v3:
time: 79.5 us; the launch traced here: 79.4 us
  Pallas kernels  77.8 us (98%)
  local copies, waits for them, and re-layouts  1.57 us (2%)
    pallas_call x1, Pallas kernels, shards(): pl.pallas_call(kernel, out_shape=jax.ShapeDtypeStruct((256, SHARE), BF),...  77.8 us

profile of v3, /device:TPU:32, one launch (start us, length us, event | category | flops | bytes accessed | tf_op | source)
XLA Modules:
  0.0 79.4 jit_solution(17292805366128498919)
XLA Ops:
  0.0 77.8 %moe.1 = bf16[256,256]{1,0:T(8,128)(2,1)} custom-call(bf16[256,256]{1,0:T(8,128)(2,1)} %tok_hbm.1, s32[2,256]{1,0:T(2,128)} %bitcast.3, f32[2,256]{1,0:T(2,128)} %bitcast.4, s32[1,256]{1,0:T(1,128)} %bitcast.5, bf16[1,2048,512]{2,1,0:T(8,128)(2,1)} %w1_hbm.1, bf16[1,512,2048]{2,1,0:T(8,128)(2,1)} %w2_hbm.1), custom_call_target="tpu_custom_call" | custom-call | flops 4294967296 | bytes 5242880 | tf_op jit(solution)/shard_map/moe/pallas_call | solution.py:263
  77.8 1.6 %copy.8 = bf16[256,256]{1,0:T(8,128)(2,1)} copy(bf16[256,256]{1,0:T(8,128)(2,1)} %moe.1) | data formatting | bytes 262144
